TPU v7x, 128 devices: a whole 4x4x4 slice. The times are simulated.
128 devices in a mesh: seq: 16 (over y, z_hi, core), head: 8 (over z_lo, x).
Axes of the slice: x: 4, y: 4, z: 4 (z_hi: 2, z_lo: 2; z = z_hi * 2 + z_lo), core: 2. Of those that a mesh axis runs over, the one named last changes fastest.
Arguments:
- query: bfloat16 [8192, 5120], P('seq', 'head'), may hold values from -6 to 6
- key_rows: bfloat16 [8192, 5120], P('seq', 'head'), may hold values from -6 to 6
- value_rows: bfloat16 [8192, 5120], P('seq', 'head'), may hold values from -6 to 6
- frame_seq: int32 [8192], replicated, may hold values from 0 to 3, never falling along the last dimension, each value on 1 to 3072 neighbouring positions
- order: int32 [32], replicated, may hold values from 0 to 31, each once
- w_out: bfloat16 [5120, 5120], P('head'), may hold values from -0.078125 to 0.078125
Outputs:
- mixed: bfloat16 [8192, 5120], P('seq', 'head')
Inputs may be any that keep to these rules, and one draw needn't show every extreme that they name: `frame_seq`: frames never fall along the sequence; each of the 4 frames holds 1 to 3072 tokens, and one holds exactly 3072. `order`: a permutation: every block number appears once.
All inputs are finite; a program needn't handle non-finite values.
Results may differ from a plain program's by a relative error of at most 0.019.
Values may be sent and summed in bfloat16 or wider, within the bound.
No kernel may reach another device: no remote copies, remote signals or barrier semaphores. Data moves between devices by JAX's collectives and lax.ppermute only.
A program may use at most 256 MiB of HBM per device.

v0:
```python
import jax
import jax.numpy as jnp
from jax import lax
from jax.sharding import PartitionSpec as P

HEAD_DIM = 128


def update(state, q_three, q_frames, k_piece, v_piece, key_frames):
    acc, run_max, total = state
    local_heads = q_three.shape[1]
    count = k_piece.shape[0]
    k_three = k_piece.reshape(count, local_heads, HEAD_DIM)
    v_three = v_piece.reshape(count, local_heads, HEAD_DIM)
    scores = jnp.einsum(
        "qhd,khd->hqk", q_three, k_three, preferred_element_type=jnp.float32
    ) * HEAD_DIM ** (-0.5)
    allowed = (key_frames[None, :] <= q_frames[:, None])[None, :, :]
    new_max = jnp.maximum(run_max, jnp.max(jnp.where(allowed, scores, -1e30), axis=2))
    expo = jnp.where(allowed, jnp.exp(scores - new_max[:, :, None]), 0.0)
    total = jnp.sum(expo, axis=2)
    added = jnp.einsum(
        "hqk,khd->hqd", expo.astype(jnp.bfloat16), v_three, preferred_element_type=jnp.float32
    )
    acc = added
    return (acc, new_max, total)


def on_device(query, key_rows, value_rows, frame_seq, order, w_out):
    rows = query.shape[0]
    blocks = order.shape[0]
    block_len = frame_seq.shape[0] // blocks
    frames_all = frame_seq.reshape(blocks, block_len)[order].reshape(-1)
    device_at = lax.axis_index("seq")
    own_frames = lax.dynamic_slice_in_dim(frames_all, device_at * rows, rows, 0)
    local_heads = query.shape[1] // HEAD_DIM
    q_three = query.reshape(rows, local_heads, HEAD_DIM)
    start_state = (
        jnp.zeros((local_heads, rows, HEAD_DIM), jnp.float32),
        jnp.full((local_heads, rows), -1e30, jnp.float32),
        jnp.zeros((local_heads, rows), jnp.float32),
    )
    k_piece = lax.all_gather(key_rows, "seq", axis=0, tiled=True)
    v_piece = lax.all_gather(value_rows, "seq", axis=0, tiled=True)
    acc, run_max, total = update(start_state, q_three, own_frames, k_piece, v_piece, frames_all)
    attended = (
        (acc / total[:, :, None])
        .transpose(1, 0, 2)
        .reshape(rows, local_heads * HEAD_DIM)
        .astype(jnp.bfloat16)
    )
    partial_sum = jnp.dot(attended, w_out, preferred_element_type=jnp.float32)
    return lax.psum_scatter(
        partial_sum.astype(jnp.bfloat16), "head", scatter_dimension=1, tiled=True
    )


def solution(mesh):
    return jax.shard_map(
        on_device,
        mesh=mesh,
        in_specs=(P("seq", "head"), P("seq", "head"), P("seq", "head"), P(), P(), P("head", None)),
        out_specs=P("seq", "head"),
        check_vma=False,
    )
```

profile of v0, /device:TPU:0, one launch (start us, length us, event | category | flops | bytes accessed | tf_op | source)
XLA Modules:
  0.0 319.2 jit_solution(1834432745027323650)
XLA Ops:
  6.5 0.0 all-gather.3.cloned.1.call-start
  6.5 2.2 copy.15
  8.7 0.0 all-gather.3.cloned.1.call-update
  8.7 0.0 all-gather.5.cloned.1.call-start
  8.8 0.7 all-gather.5.cloned.1.call-update
  9.5 0.0 reduce-scatter.4.cloned.1.call-start
  9.5 0.8 reshape.49
  10.3 0.7 compare_select_fusion
  11.0 0.6 gather_fusion
  11.6 1.3 copy.14
  12.9 0.1 dynamic_slice.3
  13.0 4.6 %broadcast_compare_fusion = pred[512,8192]{1,0:T(8,128)(4,1)} fusion(s32[8192]{0:T(1024)S(1)} %bitcast.23, s32[512]{0:T(512)S(1)} %dynamic_slice.3), kind=kLoop, calls=%fused_computation.7 | loop fusion | flops 4194304 | bytes 4229120 | tf_op jit(solution)/shard_map/le | solution.py:18
  17.7 85.5 %all-gather.3.cloned.1.call-done = bf16[8192,640]{0,1:T(8,128)(2,1)} async-done(((bf16[512,640]{0,1:T(8,128)(2,1)}), bf16[8192,640]{0,1:T(8,128)(2,1)}) %all-gather.3.cloned.1.call-update) | async-done | bytes 10485776 | tf_op jit(solution)/shard_map/all_gather | solution.py:43
  103.1 37.4 %select_reduce_fusion = (f32[5,512]{1,0:T(8,128)S(1)}, f32[5,512,8192]{2,1,0:T(8,128)}) fusion(pred[512,8192]{1,0:T(8,128)(4,1)} %broadcast_compare_fusion, bf16[512,5,128]{0,2,1:T(8,128)(2,1)S(1)} %bitcast.20, bf16[8192,5,128]{0,2,1:T(8,128)(2,1)} %bitcast.26), kind=kOutput, calls=%fused_computation.2 | convolution fusion | flops 5431621120 | bytes 99231744 | tf_op jit(solution)/shard_map/qhd,khd->hqk/dot_general | solution.py:15
  140.5 28.3 %fusion = f32[5,512]{1,0:T(8,128)S(1)} fusion(f32[5,512,8192]{2,1,0:T(8,128)} %get-tuple-element.6, f32[5,512]{1,0:T(8,128)S(1)} %broadcast_maximum_fusion, pred[512,8192]{1,0:T(8,128)(4,1)} %broadcast_compare_fusion), kind=kLoop, calls=%fused_computation.3 | loop fusion | flops 83883520 | bytes 88100864 | tf_op jit(solution)/shard_map/reduce_sum | solution.py:21
  168.8 16.5 %all-gather.5.cloned.1.call-done = bf16[8192,640]{1,0:T(8,128)(2,1)} async-done(((bf16[512,640]{1,0:T(8,128)(2,1)}), bf16[8192,640]{1,0:T(8,128)(2,1)}) %all-gather.5.cloned.1.call-update) | async-done | bytes 10485776 | tf_op jit(solution)/shard_map/all_gather | solution.py:44
  185.3 14.4 %copy.18 = bf16[8192,640]{0,1:T(8,128)(2,1)} copy(bf16[8192,640]{1,0:T(8,128)(2,1)} %all-gather.5.cloned.1.call-done) | data formatting | bytes 20971520 | tf_op jit(solution)/shard_map/all_gather | solution.py:44
  199.7 33.1 %divide_convert_fusion = bf16[512,5,128]{0,2,1:T(8,128)(2,1)S(1)} fusion(bf16[8192,5,128]{0,2,1:T(8,128)(2,1)} %bitcast.19, f32[5,512,8192]{2,1,0:T(8,128)} %get-tuple-element.6, f32[5,512]{1,0:T(8,128)S(1)} %broadcast_maximum_fusion, pred[512,8192]{1,0:T(8,128)(4,1)} %broadcast_compare_fusion, f32[512,5]{0,1:T(8,128)S(1)} %bitcast.25), kind=kOutput, calls=%fused_computation.10 | convolution fusion | flops 5453250560 | bytes 99241984 | tf_op jit(solution)/shard_map/hqk,khd->hqd/dot_general | solution.py:22
  232.8 8.9 %convolution_convert_fusion = bf16[512,5120]{1,0:T(8,128)(2,1)} fusion(bf16[512,640]{0,1:T(8,128)(2,1)S(1)} %bitcast.27, bf16[640,5120]{1,0:T(8,128)(2,1)} %param.11), kind=kOutput, calls=%fused_computation.8 | convolution fusion | flops 3358064640 | bytes 12451840 | tf_op jit(solution)/shard_map/dot_general | solution.py:52
  241.8 7.9 %copy.21 = bf16[512,5120]{0,1:T(8,128)(2,1)} copy(bf16[512,5120]{1,0:T(8,128)(2,1)} %convolution_convert_fusion) | data formatting | bytes 10485760
  249.7 0.0 reduce-scatter.4.cloned.1.call-update
  249.7 60.8 %reduce-scatter.4.cloned.1.call-done = bf16[640,512]{1,0:T(8,128)(2,1)} async-done(((bf16[5120,512]{1,0:T(8,128)(2,1)}), bf16[640,512]{1,0:T(8,128)(2,1)}) %reduce-scatter.4.cloned.1.call-update) | async-done | bytes 655376
  310.5 2.2 copy.22
  (3 shorter events, 0.0 us)
Async XLA Ops:
  6.5 96.6 %all-gather.3.cloned.1.call-start = ((), (), s32[]{:S(2)}) async-start(), calls=%async_computation.1 | async-start | bytes 11141120 | tf_op jit(solution)/shard_map/all_gather | solution.py:43
  8.7 176.6 %all-gather.5.cloned.1.call-start = ((), (), s32[]{:S(2)}) async-start(), calls=%async_computation.2 | async-start | bytes 11141120 | tf_op jit(solution)/shard_map/all_gather | solution.py:44
  9.5 301.0 %reduce-scatter.4.cloned.1.call-start = ((), (), s32[]{:S(2)}) async-start(), calls=%async_computation.3 | async-start | bytes 5898240
Sparse Core Ops, SparseCore 0:
  9.6 93.4 all-gather.2
  105.5 79.7 all-gather.4
  249.8 60.6 reduce-scatter.3
where the time goes:
time: 321 us; the launch traced here: 319 us
  waiting for transfers between devices  164 us (51%)
  matrix products  79.5 us (25%)
  other arithmetic  33.5 us (10%)
  local copies, waits for them, and re-layouts  29.4 us (9%)
  between operations  13.1 us (4%)
    all_gather x1, waiting for transfers between devices, on_device(): k_piece = lax.all_gather(key_rows, 'seq', axis=0, tiled=True)  85.5 us
    unnamed x4, waiting for transfers between devices  61.5 us
    dot_general x1, matrix products, update(): jnp.einsum('qhd,khd->hqk', q_three, k_three, preferred_element_type=jnp.f...  37.4 us
    dot_general x1, matrix products, update(): jnp.einsum('hqk,khd->hqd', expo.astype(jnp.bfloat16), v_three, preferred_...  33.1 us
    reduce_sum x1, other arithmetic, update(): total = jnp.sum(expo, axis=2)  28.3 us
    all_gather x1, waiting for transfers between devices, on_device(): v_piece = lax.all_gather(value_rows, 'seq', axis=0, tiled=True)  16.5 us
    all_gather x1, local copies, waits for them, and re-layouts, on_device(): v_piece = lax.all_gather(value_rows, 'seq', axis=0, tiled=True)  14.4 us
    unnamed x5, local copies, waits for them, and re-layouts  13.6 us
  transfers between devices with their start and end apart: 3, of which 3 were waited for; matrix products, arithmetic and copies ran while one was open for 23% of the time, Pallas kernels for 0%

commit v1 on v0

v1 whole, which is shorter than its diff:
```python
import functools
import math

import jax
import jax.numpy as jnp
from jax import lax
from jax.experimental import pallas as pl
from jax.experimental.pallas import tpu as pltpu
from jax.sharding import PartitionSpec as P

HEAD_DIM = 128
BLOCK = 256
FRAMES = 4
BIG = 1e30
SCALE = HEAD_DIM ** (-0.5) * math.log2(math.e)
KEYS_STEP = 512
MIB = 1024 * 1024


def linear(y, zh, core, zl, x):
    return (((y % 4) * 2 + zh) * 2 + core) * 8 + zl * 4 + x % 4


def moved(move):
    pairs = []
    for y in range(4):
        for zh in range(2):
            for core in range(2):
                for zl in range(2):
                    for x in range(4):
                        at = (y, zh, core, zl, x)
                        pairs.append((linear(*at), linear(*move(*at))))
    return pairs


CORE = moved(lambda y, zh, core, zl, x: (y, zh, 1 - core, zl, x))
Z_HI = moved(lambda y, zh, core, zl, x: (y, 1 - zh, core, zl, x))


def y_shift(step):
    return moved(lambda y, zh, core, zl, x: (y + step, zh, core, zl, x))


def send(value, pairs):
    return lax.ppermute(value, ("seq", "head"), pairs)


def three_pieces(value):
    high = value.astype(jnp.bfloat16)
    rest = value - high.astype(jnp.float32)
    middle = rest.astype(jnp.bfloat16)
    low = (rest - middle.astype(jnp.float32)).astype(jnp.bfloat16)
    return high, middle, low


def attention_kernel(
    first, heads, blocks_total, order_ref, frames_ref, *refs
):
    q_parts, kv_parts = refs[:4], refs[4:8]
    keep_ref, give_ref = refs[8:10]
    q_all, k_all, v_all, mask_all, top_ref, acc_ref, base_ref, kv_sem, q_sem = refs[10:]
    width = heads * HEAD_DIM
    seq_at = lax.axis_index("seq")
    y_at = lax.shift_right_logical(seq_at, 2)
    column_at = lax.rem(seq_at, 4)
    tokens = blocks_total * BLOCK

    ends = []
    for f in range(FRAMES - 1):
        below = jnp.where(frames_ref[...] <= f, 1.0, 0.0)
        ends.append(jnp.sum(below).astype(jnp.int32))
    ends.append(jnp.int32(tokens))

    bases = []
    for part in range(4):
        row = lax.rem(y_at + part, 4)
        for half in range(2):
            bases.append(order_ref[row * 8 + column_at * 2 + half] * BLOCK)
    copies = []
    for i in range(8):
        rank = jnp.int32(0)
        for j in range(8):
            if j != i:
                rank = rank + jnp.where(bases[j] < bases[i], 1, 0)
        base_ref[rank] = bases[i]
        rows = pl.ds((i % 2) * BLOCK, BLOCK)
        to = pl.ds(pl.multiple_of(rank * BLOCK, BLOCK), BLOCK)
        part = kv_parts[i // 2]
        for n, (dst, at) in enumerate(((k_all, 0), (v_all, width))):
            copy = pltpu.make_async_copy(
                part.at[rows, pl.ds(at, width)], dst.at[to, :], kv_sem.at[2 * i + n]
            )
            copy.start()
            copies.append(copy)
    for part in range(4):
        copy = pltpu.make_async_copy(
            q_parts[part].at[:, pl.ds(first * HEAD_DIM, width)],
            q_all.at[pl.ds(part * 512, 512), :],
            q_sem.at[part],
        )
        copy.start()
        copies.append(copy)

    lane = lax.broadcasted_iota(jnp.int32, (BLOCK, HEAD_DIM), 1)
    offset = lax.broadcasted_iota(jnp.int32, (BLOCK, HEAD_DIM), 0)
    lane_end = jnp.where(
        lane == 0, ends[0], jnp.where(lane == 1, ends[1], jnp.where(lane == 2, ends[2], tokens))
    )
    lane_start = jnp.where(
        lane == 0, 0, jnp.where(lane == 1, ends[0], jnp.where(lane == 2, ends[1], ends[2]))
    )
    for slot in range(8):
        token = base_ref[slot] + offset
        hidden = (token >= lane_end) & (lane < FRAMES)
        mask_all[pl.ds(slot * BLOCK, BLOCK), :] = jnp.where(hidden, -BIG, 0.0).astype(jnp.bfloat16)
    for copy in copies:
        copy.wait()

    ones = jnp.ones((KEYS_STEP, HEAD_DIM), jnp.bfloat16)

    def one_block(index, out_ref, out_at, order_at):
        base = order_ref[order_at] * BLOCK
        last = base + (BLOCK - 1)
        limit = jnp.where(
            last < ends[0], ends[0],
            jnp.where(last < ends[1], ends[1], jnp.where(last < ends[2], ends[2], tokens)),
        )
        count = jnp.int32(0)
        for slot in range(8):
            count = count + jnp.where(base_ref[slot] < limit, 1, 0)
        steps = jnp.maximum(lax.div(count * BLOCK + (KEYS_STEP - 1), KEYS_STEP), 1)
        token = base + offset
        own = (token >= lane_start) & (token < lane_end) & (lane < FRAMES)
        own_frame = jnp.where(own, 1.0, 0.0).astype(jnp.bfloat16)
        top_ref[...] = jnp.full(top_ref.shape, -2.0 * BIG, jnp.float32)
        acc_ref[...] = jnp.zeros(acc_ref.shape, jnp.float32)
        q_rows = pl.ds(pl.multiple_of(index * BLOCK, BLOCK), BLOCK)

        def step(at, carry):
            rows = pl.ds(pl.multiple_of(at * KEYS_STEP, KEYS_STEP), KEYS_STEP)
            hidden = mask_all[rows, :]
            for h in range(heads):
                cols = pl.ds(h * HEAD_DIM, HEAD_DIM)
                q_ext = jnp.concatenate([q_all[q_rows, cols], own_frame], axis=1)
                k_ext = jnp.concatenate([k_all[rows, cols], hidden], axis=1)
                scores = lax.dot_general(
                    q_ext, k_ext, (((1,), (1,)), ((), ())), preferred_element_type=jnp.float32
                )
                before = top_ref[h]
                top = jnp.maximum(before[:, :1], jnp.max(scores, axis=1, keepdims=True))
                expo = jnp.exp2((scores - top) * SCALE).astype(jnp.bfloat16)
                shrink = jnp.exp2((before[:, :1] - top) * SCALE)
                v_ext = jnp.concatenate([v_all[rows, cols], ones], axis=1)
                added = jnp.dot(expo, v_ext, preferred_element_type=jnp.float32)
                acc_ref[h] = acc_ref[h] * shrink + added
                top_ref[h] = jnp.broadcast_to(top, (BLOCK, HEAD_DIM))
            return carry

        lax.fori_loop(0, steps, step, 0)
        out_rows = pl.ds(pl.multiple_of(out_at * BLOCK, BLOCK), BLOCK)
        stats = jnp.zeros((BLOCK, HEAD_DIM), jnp.bfloat16)
        for h in range(heads):
            total = acc_ref[h, :, HEAD_DIM:]
            out_ref[out_rows, pl.ds(h * HEAD_DIM, HEAD_DIM)] = (
                acc_ref[h, :, :HEAD_DIM] / total
            ).astype(jnp.bfloat16)
            log_sum = top_ref[h] * SCALE + jnp.log2(total)
            for n, piece in enumerate(three_pieces(log_sum)):
                stats = jnp.where(lane == 3 * h + n, piece, stats)
        out_ref[out_rows, pl.ds(width, HEAD_DIM)] = stats

    def blocks(n, carry):
        part = lax.div(n, 2)
        half = lax.rem(n, 2)
        flip_core = lax.rem(part, 2)
        flip_z = lax.div(part, 2)
        core = lax.rem(column_at, 2)
        zh = lax.div(column_at, 2)
        core_at = core + flip_core - 2 * core * flip_core
        z_at = zh + flip_z - 2 * zh * flip_z
        order_at = y_at * 8 + z_at * 4 + core_at * 2 + half
        out_at = flip_z * 2 + half

        @pl.when(flip_core == 0)
        def _():
            one_block(n, keep_ref, out_at, order_at)

        @pl.when(flip_core == 1)
        def _():
            one_block(n, give_ref, out_at, order_at)

        return carry

    lax.fori_loop(0, 8, blocks, 0)


def attention(first, heads, order, frames, q_parts, kv_parts):
    width = heads * HEAD_DIM
    part_shape = jax.ShapeDtypeStruct((1024, width + HEAD_DIM), jnp.bfloat16)
    any_spec = pl.BlockSpec(memory_space=pl.ANY)
    vmem_spec = pl.BlockSpec(memory_space=pltpu.VMEM)
    return pl.pallas_call(
        functools.partial(attention_kernel, first, heads, order.shape[0]),
        out_shape=(part_shape, part_shape),
        in_specs=[pl.BlockSpec(memory_space=pltpu.SMEM), vmem_spec] + [any_spec] * 8,
        out_specs=(vmem_spec, vmem_spec),
        scratch_shapes=[
            pltpu.VMEM((2048, width), jnp.bfloat16),
            pltpu.VMEM((2048, width), jnp.bfloat16),
            pltpu.VMEM((2048, width), jnp.bfloat16),
            pltpu.VMEM((2048, HEAD_DIM), jnp.bfloat16),
            pltpu.VMEM((heads, BLOCK, HEAD_DIM), jnp.float32),
            pltpu.VMEM((heads, BLOCK, 2 * HEAD_DIM), jnp.float32),
            pltpu.SMEM((8,), jnp.int32),
            pltpu.SemaphoreType.DMA((16,)),
            pltpu.SemaphoreType.DMA((4,)),
        ],
        compiler_params=pltpu.CompilerParams(vmem_limit_bytes=40 * MIB),
        cost_estimate=pl.CostEstimate(
            flops=heads * 2048 * 2048 * 128 * 8, bytes_accessed=8 * MIB, transcendentals=0
        ),
    )(order, frames, *q_parts, *kv_parts)


def merged(heads, mine, theirs):
    lane_at = heads * HEAD_DIM
    values, sums = [], []
    for h in range(heads):
        logs = []
        for ref in (mine, theirs):
            pieces = [
                ref[:, pl.ds(lane_at + 3 * h + n, 1)].astype(jnp.float32) for n in range(3)
            ]
            logs.append(pieces[0] + pieces[1] + pieces[2])
        top = jnp.maximum(logs[0], logs[1])
        first, second = jnp.exp2(logs[0] - top), jnp.exp2(logs[1] - top)
        total = first + second
        cols = pl.ds(h * HEAD_DIM, HEAD_DIM)
        values.append(
            mine[:, cols].astype(jnp.float32) * (first / total)
            + theirs[:, cols].astype(jnp.float32) * (second / total)
        )
        sums.append(top + jnp.log2(total))
    return values, sums


def merge_kernel(heads, with_sums, mine, theirs, out):
    values, sums = merged(heads, mine, theirs)
    for h in range(heads):
        out[:, pl.ds(h * HEAD_DIM, HEAD_DIM)] = values[h].astype(jnp.bfloat16)
    if with_sums:
        rows = out.shape[0]
        lane = lax.broadcasted_iota(jnp.int32, (rows, HEAD_DIM), 1)
        stats = jnp.zeros((rows, HEAD_DIM), jnp.bfloat16)
        for h in range(heads):
            for n, piece in enumerate(three_pieces(sums[h])):
                stats = jnp.where(lane == 3 * h + n, piece, stats)
        out[:, pl.ds(heads * HEAD_DIM, HEAD_DIM)] = stats


def merge(heads, mine, theirs, with_sums):
    rows = mine.shape[0]
    width = heads * HEAD_DIM + (HEAD_DIM if with_sums else 0)
    tile = 256
    spec = pl.BlockSpec((tile, heads * HEAD_DIM + HEAD_DIM), lambda i: (i, 0))
    return pl.pallas_call(
        functools.partial(merge_kernel, heads, with_sums),
        out_shape=jax.ShapeDtypeStruct((rows, width), jnp.bfloat16),
        grid=(rows // tile,),
        in_specs=[spec, spec],
        out_specs=pl.BlockSpec((tile, width), lambda i: (i, 0)),
        compiler_params=pltpu.CompilerParams(vmem_limit_bytes=16 * MIB),
        cost_estimate=pl.CostEstimate(
            flops=rows * width * 8, bytes_accessed=rows * width * 6, transcendentals=0
        ),
    )(mine, theirs)


CHUNKS = ((0, 5),)


def on_device(query, key_rows, value_rows, frame_seq, order, w_out):
    frames = frame_seq.reshape(64, 128)
    q_core = send(query, CORE)
    q_z = send(query, Z_HI)
    q_both = send(q_z, CORE)
    q_parts = (query, q_core, q_z, q_both)
    attended = []
    for first, heads in CHUNKS:
        cols = slice(first * HEAD_DIM, (first + heads) * HEAD_DIM)
        kv = jnp.concatenate([key_rows[:, cols], value_rows[:, cols]], axis=1)
        kv_parts = (kv, send(kv, y_shift(-1)), send(kv, y_shift(2)), send(kv, y_shift(1)))
        keep, give = attention(first, heads, order, frames, q_parts, kv_parts)
        both = merge(heads, keep, send(give, CORE), True)
        got = send(both[512:], Z_HI)
        attended.append(merge(heads, both[:512], got, False))
    joined = jnp.concatenate(attended, axis=1)
    partial_sum = jnp.dot(joined, w_out, preferred_element_type=jnp.float32)
    return lax.psum_scatter(
        partial_sum.astype(jnp.bfloat16), "head", scatter_dimension=1, tiled=True
    )


def solution(mesh):
    return jax.shard_map(
        on_device,
        mesh=mesh,
        in_specs=(P("seq", "head"), P("seq", "head"), P("seq", "head"), P(), P(), P("head", None)),
        out_specs=P("seq", "head"),
        check_vma=False,
    )
```

time: 321 us -> 239 us (0.74)
  matrix products: 79.5 us -> 6.02 us
  Pallas kernels: 0 us -> 56.4 us
  other arithmetic: 33.5 us -> 0.01 us
  waiting for transfers between devices: 164 us -> 139 us
  local copies, waits for them, and re-layouts: 29.4 us -> 11.5 us
  starting transfers between devices: 0.08 us -> 13.8 us
    all_gather x2 -> x0, waiting for transfers between devices: 102 us -> none  [the longest x1 85.5 us: on_device(): k_piece = lax.all_gather(key_rows, 'seq', axis=0, tiled=True)]
    ppermute x0 -> x8, waiting for transfers between devices: none -> 76.2 us  [send(): return lax.ppermute(value, ('seq', 'head'), pairs)]
    dot_general x3 -> x1, matrix products: 79.5 us -> 6.02 us  [on_device(): partial_sum = jnp.dot(joined, w_out, preferred_element_type=jnp.float32)]
    pallas_call x0 -> x3, Pallas kernels: none -> 56.4 us  [the longest x1 51.8 us: attention(): pl.pallas_call(functools.partial(attention_kernel, first, heads, order.sh...]
    reduce_sum x1 -> x0, other arithmetic: 28.3 us -> none  [update(): total = jnp.sum(expo, axis=2)]
    all_gather x1 -> x0, local copies, waits for them, and re-layouts: 14.4 us -> none  [on_device(): v_piece = lax.all_gather(value_rows, 'seq', axis=0, tiled=True)]
    ppermute x0 -> x8, starting transfers between devices: none -> 13.8 us  [send(): return lax.ppermute(value, ('seq', 'head'), pairs)]
    le x1 -> x0, other arithmetic: 4.63 us -> none  [update(): allowed = (key_frames[None, :] <= q_frames[:, None])[None, :, :]]
  transfers between devices with their start and end apart: 3 -> 9, of which waited for: 3 -> 7; matrix products, arithmetic and copies ran while one was open for 23% -> 1% of each run, Pallas kernels for 0% -> 0%
where the time goes in v1:
time: 239 us; the launch traced here: 240 us
  waiting for transfers between devices  139 us (58%)
  Pallas kernels  56.4 us (24%)
  starting transfers between devices  13.8 us (6%)
  between operations  13.5 us (6%)
  local copies, waits for them, and re-layouts  11.5 us (5%)
  matrix products  6.02 us (3%)
    ppermute x8, waiting for transfers between devices, send(): return lax.ppermute(value, ('seq', 'head'), pairs)  76.2 us
    unnamed x2, waiting for transfers between devices  62.5 us
    pallas_call x1, Pallas kernels, attention(): pl.pallas_call(functools.partial(attention_kernel, first, heads, order.sh...  51.8 us
    ppermute x8, starting transfers between devices, send(): return lax.ppermute(value, ('seq', 'head'), pairs)  13.8 us
    unnamed x15, local copies, waits for them, and re-layouts  11.3 us
    dot_general x1, matrix products, on_device(): partial_sum = jnp.dot(joined, w_out, preferred_element_type=jnp.float32)  6.02 us
  transfers between devices with their start and end apart: 9, of which 7 were waited for; matrix products, arithmetic and copies ran while one was open for 1% of the time, Pallas kernels for 0%

profile of v1, /device:TPU:0, one launch (start us, length us, event | category | flops | bytes accessed | tf_op | source)
XLA Modules:
  0.0 239.8 jit_solution(18190132942819330683)
XLA Ops:
  6.5 0.0 reduce-scatter.4.cloned.1.call-start
  6.6 4.0 %collective-permute-start.1 = (bf16[512,640]{1,0:T(8,128)(2,1)}, bf16[512,640]{1,0:T(8,128)(2,1)S(1)}, u32[]{:S(2)}, u32[]{:S(2)}) collective-permute-start(bf16[512,640]{1,0:T(8,128)(2,1)} %refs_0_.1), channel_id=1, source_target_pairs={{0,16},{1,17},{2,18},{3,19},{4,20},{5,21},{6,22},{7,23},{8,24},{9,... | collective-permute-start | bytes 1966088 | tf_op jit(solution)/shard_map/ppermute | solution.py:45
  10.6 1.1 constant_dynamic-update-slice_fusion.1
  11.8 0.0 copy-done.3
  11.8 0.0 slice-start
  11.8 0.1 constant_dynamic-update-slice_fusion.refs_4_
  11.9 1.6 collective-permute-start.5
  13.5 2.9 %collective-permute-start.4 = (bf16[512,1280]{1,0:T(8,128)(2,1)S(1)}, bf16[512,1280]{1,0:T(8,128)(2,1)S(1)}, u32[]{:S(2)}, u32[]{:S(2)}) collective-permute-start(bf16[512,1280]{1,0:T(8,128)(2,1)S(1)} %constant_dynamic-update-slice_fusion.refs_4_), channel_id=1, source_target_pairs={{0,64},{1,65},{2,66},{3,67},{4,68},{5,69},{6,70},{7,71},{8,72},{9,... | collective-permute-start | bytes 3932168 | tf_op jit(solution)/shard_map/ppermute | solution.py:45
  16.4 1.3 collective-permute-start.3
  17.8 0.0 copy-done
  17.8 0.0 collective-permute-start
  17.8 7.8 %collective-permute-done.1.refs_2_ = bf16[512,640]{1,0:T(8,128)(2,1)S(1)} collective-permute-done((bf16[512,640]{1,0:T(8,128)(2,1)}, bf16[512,640]{1,0:T(8,128)(2,1)S(1)}, u32[]{:S(2)}, u32[]{:S(2)}) %collective-permute-start.1) | collective-permute-done | bytes 655392 | tf_op jit(solution)/shard_map/ppermute | solution.py:45
  25.6 0.0 collective-permute-start.2
  25.6 0.0 collective-permute-done.refs_1_
  25.6 2.1 collective-permute-done.2.refs_3_
  27.7 16.1 %collective-permute-done.5.refs_7_ = bf16[512,1280]{1,0:T(8,128)(2,1)S(1)} collective-permute-done((bf16[512,1280]{1,0:T(8,128)(2,1)S(1)}, bf16[512,1280]{1,0:T(8,128)(2,1)S(1)}, u32[]{:S(2)}, u32[]{:S(2)}) %collective-permute-start.5) | collective-permute-done | bytes 1310752 | tf_op jit(solution)/shard_map/ppermute | solution.py:45
  43.8 29.0 %collective-permute-done.4.refs_6_ = bf16[512,1280]{1,0:T(8,128)(2,1)S(1)} collective-permute-done((bf16[512,1280]{1,0:T(8,128)(2,1)S(1)}, bf16[512,1280]{1,0:T(8,128)(2,1)S(1)}, u32[]{:S(2)}, u32[]{:S(2)}) %collective-permute-start.4) | collective-permute-done | bytes 1310752 | tf_op jit(solution)/shard_map/ppermute | solution.py:45
  72.7 0.0 collective-permute-done.3.refs_5_
  72.8 0.0 slice-start.1
  72.8 51.8 %shard_map.64 = (bf16[1024,768]{1,0:T(8,128)(2,1)S(1)}, bf16[1024,768]{1,0:T(8,128)(2,1)S(1)}) custom-call(s32[32]{0:T(128)S(1)} %copy-done.2, s32[64,128]{1,0:T(8,128)S(1)} %bitcast.5, bf16[512,640]{1,0:T(8,128)(2,1)S(1)} %copy-done, bf16[512,640]{1,0:T(8,128)(2,1)S(1)} %collective-permute-done.refs_1_, ...), custom_call_target="tpu_custom_call" | custom-call | flops 21474836480 | bytes 8388608 | tf_op jit(solution)/shard_map/pallas_call | solution.py:202
  124.5 0.1 collective-permute-start.6
  124.6 3.4 %collective-permute-done.6.theirs = bf16[1024,768]{1,0:T(8,128)(2,1)S(1)} collective-permute-done((bf16[1024,768]{1,0:T(8,128)(2,1)S(1)}, bf16[1024,768]{1,0:T(8,128)(2,1)S(1)}, u32[]{:S(2)}, u32[]{:S(2)}) %collective-permute-start.6) | collective-permute-done | bytes 1572896 | tf_op jit(solution)/shard_map/ppermute | solution.py:45
  128.0 3.4 %shard_map.65 = bf16[1024,768]{1,0:T(8,128)(2,1)S(1)} custom-call(bf16[1024,768]{1,0:T(8,128)(2,1)S(1)} %get-tuple-element.7.mine, bf16[1024,768]{1,0:T(8,128)(2,1)S(1)} %collective-permute-done.6.theirs), custom_call_target="tpu_custom_call" | custom-call | flops 6291456 | bytes 4718592 | tf_op jit(solution)/shard_map/pallas_call | solution.py:266
  131.5 0.1 fusion
  131.6 3.8 %collective-permute-start.7 = (bf16[512,768]{1,0:T(8,128)(2,1)S(1)}, bf16[512,768]{1,0:T(8,128)(2,1)S(1)}, u32[]{:S(2)}, u32[]{:S(2)}) collective-permute-start(bf16[512,768]{1,0:T(8,128)(2,1)S(1)} %get-tuple-element.9), channel_id=1, source_target_pairs={{0,16},{1,17},{2,18},{3,19},{4,20},{5,21},{6,22},{7,23},{8,24},{9,... | collective-permute-start | bytes 2359304 | tf_op jit(solution)/shard_map/ppermute | solution.py:45
  135.3 17.8 %collective-permute-done.7.theirs = bf16[512,768]{1,0:T(8,128)(2,1)S(1)} collective-permute-done((bf16[512,768]{1,0:T(8,128)(2,1)S(1)}, bf16[512,768]{1,0:T(8,128)(2,1)S(1)}, u32[]{:S(2)}, u32[]{:S(2)}) %collective-permute-start.7) | collective-permute-done | bytes 786464 | tf_op jit(solution)/shard_map/ppermute | solution.py:45
  153.2 1.2 shard_map.66
  154.4 6.0 %convolution_convert_fusion = bf16[512,5120]{1,0:T(8,128)(2,1)} fusion(bf16[512,640]{1,0:T(8,128)(2,1)S(1)} %shard_map.66, bf16[640,5120]{1,0:T(8,128)(2,1)S(1)} %bitcast.9), kind=kOutput, calls=%fused_computation | convolution fusion | flops 3358064640 | bytes 12451840 | tf_op jit(solution)/shard_map/dot_general | solution.py:298
  160.4 7.9 %copy.7 = bf16[512,5120]{0,1:T(8,128)(2,1)} copy(bf16[512,5120]{1,0:T(8,128)(2,1)} %convolution_convert_fusion) | data formatting | bytes 10485760
  168.3 0.0 reduce-scatter.4.cloned.1.call-update
  168.4 62.5 %reduce-scatter.4.cloned.1.call-done = bf16[640,512]{1,0:T(8,128)(2,1)} async-done(((bf16[5120,512]{1,0:T(8,128)(2,1)}), bf16[640,512]{1,0:T(8,128)(2,1)}) %reduce-scatter.4.cloned.1.call-update) | async-done | bytes 655376
  230.8 2.2 copy.8
  (9 shorter events, 0.0 us)
Async XLA Ops:
  6.5 11.3 %copy-start = (bf16[512,640]{1,0:T(8,128)(2,1)S(1)}, bf16[512,640]{1,0:T(8,128)(2,1)}, u32[]{:S(2)}) copy-start(bf16[512,640]{1,0:T(8,128)(2,1)} %refs_0_.1) | copy-start | bytes 1966084
  6.5 5.2 %copy-start.3 = (bf16[512,640]{1,0:T(8,128)(2,1)S(1)}, bf16[512,640]{1,0:T(8,128)(2,1)}, u32[]{:S(2)}) copy-start(bf16[512,640]{1,0:T(8,128)(2,1)} %param.8) | copy-start | bytes 1966084
  6.5 66.2 %copy-start.2 = (s32[32]{0:T(128)S(1)}, s32[32]{0:T(128)}, u32[]{:S(2)}) copy-start(s32[32]{0:T(128)} %order_ref.1) | copy-start | bytes 388
  6.5 66.2 %copy-start.1 = (s32[8192]{0:T(1024)S(1)}, s32[8192]{0:T(1024)}, u32[]{:S(2)}) copy-start(s32[8192]{0:T(1024)} %param.9) | copy-start | bytes 98308
  6.5 224.3 %reduce-scatter.4.cloned.1.call-start = ((), (), s32[]{:S(2)}) async-start(), calls=%async_computation.1 | async-start | bytes 5898240
  6.6 19.0 %collective-permute-start.1 = (bf16[512,640]{1,0:T(8,128)(2,1)}, bf16[512,640]{1,0:T(8,128)(2,1)S(1)}, u32[]{:S(2)}, u32[]{:S(2)}) collective-permute-start(bf16[512,640]{1,0:T(8,128)(2,1)} %refs_0_.1), channel_id=1, source_target_pairs={{0,16},{1,17},{2,18},{3,19},{4,20},{5,21},{6,22},{7,23},{8,24},{9,... | collective-permute-start | bytes 1966088 | tf_op jit(solution)/shard_map/ppermute | solution.py:45
  11.8 142.6 %slice-start = ((s8[6553600]{0:T(1024)(128)(4,1)}), s8[4194304]{0:T(1024)(128)(4,1)S(1)}, s32[]{:S(2)}) async-start(s8[6553600]{0:T(1024)(128)(4,1)} %bitcast.8), calls=%async_computation.2 | async-start | bytes 8388608
  11.9 31.9 %collective-permute-start.5 = (bf16[512,1280]{1,0:T(8,128)(2,1)S(1)}, bf16[512,1280]{1,0:T(8,128)(2,1)S(1)}, u32[]{:S(2)}, u32[]{:S(2)}) collective-permute-start(bf16[512,1280]{1,0:T(8,128)(2,1)S(1)} %constant_dynamic-update-slice_fusion.refs_4_), channel_id=1, source_target_pairs={{0,32},{1,33},{2,34},{3,35},{4,36},{5,37},{6,38},{7,39},{8,40},{9,... | collective-permute-start | bytes 3932168 | tf_op jit(solution)/shard_map/ppermute | solution.py:45
  13.5 59.2 %collective-permute-start.4 = (bf16[512,1280]{1,0:T(8,128)(2,1)S(1)}, bf16[512,1280]{1,0:T(8,128)(2,1)S(1)}, u32[]{:S(2)}, u32[]{:S(2)}) collective-permute-start(bf16[512,1280]{1,0:T(8,128)(2,1)S(1)} %constant_dynamic-update-slice_fusion.refs_4_), channel_id=1, source_target_pairs={{0,64},{1,65},{2,66},{3,67},{4,68},{5,69},{6,70},{7,71},{8,72},{9,... | collective-permute-start | bytes 3932168 | tf_op jit(solution)/shard_map/ppermute | solution.py:45
  16.4 56.3 %collective-permute-start.3 = (bf16[512,1280]{1,0:T(8,128)(2,1)S(1)}, bf16[512,1280]{1,0:T(8,128)(2,1)S(1)}, u32[]{:S(2)}, u32[]{:S(2)}) collective-permute-start(bf16[512,1280]{1,0:T(8,128)(2,1)S(1)} %constant_dynamic-update-slice_fusion.refs_4_), channel_id=1, source_target_pairs={{0,96},{1,97},{2,98},{3,99},{4,100},{5,101},{6,102},{7,103},{8,104... | collective-permute-start | bytes 3932168 | tf_op jit(solution)/shard_map/ppermute | solution.py:45
  17.8 7.8 %collective-permute-start = (bf16[512,640]{1,0:T(8,128)(2,1)S(1)}, bf16[512,640]{1,0:T(8,128)(2,1)S(1)}, u32[]{:S(2)}, u32[]{:S(2)}) collective-permute-start(bf16[512,640]{1,0:T(8,128)(2,1)S(1)} %copy-done), channel_id=1, source_target_pairs={{0,8},{1,9},{2,10},{3,11},{4,12},{5,13},{6,14},{7,15},{8,0},{9,1},... | collective-permute-start | bytes 1966088 | tf_op jit(solution)/shard_map/ppermute | solution.py:45
  25.6 2.1 collective-permute-start.2
  72.8 81.6 %slice-start.1 = ((s8[6553600]{0:T(1024)(128)(4,1)}), s8[2359296]{0:T(1024)(128)(4,1)S(1)}, s32[]{:S(2)}) async-start(s8[6553600]{0:T(1024)(128)(4,1)} %bitcast.8), calls=%async_computation.3 | async-start | bytes 4718592
  124.5 3.5 %collective-permute-start.6 = (bf16[1024,768]{1,0:T(8,128)(2,1)S(1)}, bf16[1024,768]{1,0:T(8,128)(2,1)S(1)}, u32[]{:S(2)}, u32[]{:S(2)}) collective-permute-start(bf16[1024,768]{1,0:T(8,128)(2,1)S(1)} %get-tuple-element.8), channel_id=1, source_target_pairs={{0,8},{1,9},{2,10},{3,11},{4,12},{5,13},{6,14},{7,15},{8,0},{9,1},... | collective-permute-start | bytes 4718600 | tf_op jit(solution)/shard_map/ppermute | solution.py:45
  131.6 21.6 %collective-permute-start.7 = (bf16[512,768]{1,0:T(8,128)(2,1)S(1)}, bf16[512,768]{1,0:T(8,128)(2,1)S(1)}, u32[]{:S(2)}, u32[]{:S(2)}) collective-permute-start(bf16[512,768]{1,0:T(8,128)(2,1)S(1)} %get-tuple-element.9), channel_id=1, source_target_pairs={{0,16},{1,17},{2,18},{3,19},{4,20},{5,21},{6,22},{7,23},{8,24},{9,... | collective-permute-start | bytes 2359304 | tf_op jit(solution)/shard_map/ppermute | solution.py:45
Sparse Core Ops, SparseCore 0:
  168.5 62.2 reduce-scatter.3
